TPU v7x, 32 devices: a whole 2x2x4 slice. The times are simulated.
32 devices in a mesh: parts: 2 (over y), tile: 4 (over z), slide: 4 (over x, core), chan: 1.
Axes of the slice: x: 2, y: 2, z: 4, core: 2. Of those that a mesh axis runs over, the one named last changes fastest.
Arguments:
- residual_pool: bfloat16 [16, 20, 7, 7, 2048], P(('parts', 'slide'), 'tile', None, None, 'chan'), parts along dimension 0, may hold values from -8 to 8
- inner_pool: bfloat16 [16, 20, 7, 7, 2048], P(('parts', 'slide'), 'tile', None, None, 'chan'), parts along dimension 0, may hold values from -6 to 6
- window_index: int32 [16, 16], P(('parts', 'slide'), 'tile'), parts along dimension 0, may hold values from 0 to 4, as said below
- labels: int32 [16], P(('parts', 'slide')), parts along dimension 0, may hold values from 0 to 3
- group_weight: bfloat16 [3, 3, 64, 2048], P(None, None, None, 'chan'), may hold values from -2 to 2
- expand_weight: bfloat16 [2048, 2048], P(None, 'chan'), may hold values from -0.125 to 0.125
- attn_proj: bfloat16 [2, 2048, 256], P(None, 'chan'), may hold values from -0.5 to 0.5
- attn_vector: bfloat16 [256, 8], replicated, may hold values from -0.29882812 to 0.29882812
- classifier: bfloat16 [8, 2048, 4], P(None, 'chan'), may hold values from -0.046875 to 0.046875
Outputs:
- slide_loss: float32 [16], P(('parts', 'slide')), parts along dimension 0
- dir_w2: bfloat16 [6, 3, 64, 2048], P('parts', None, None, 'chan'), parts along dimension 0
- dir_w3: float32 [4096, 2048], P(('parts', 'tile', 'slide'), 'chan'), parts along dimension 0
- dir_proj: bfloat16 [4, 2048, 256], P('parts', 'chan'), parts along dimension 0
- dir_vector: float32 [512, 8], P('parts'), parts along dimension 0
- dir_class: float32 [16, 2048, 4], P('parts', 'chan'), parts along dimension 0
There are 2 independent parts, one for each index of `parts`. A program takes and returns all parts, laid end to end along the dimension named above; an argument that names none is the same for every part. Nothing has to cross between parts.
Inputs may be any that keep to these rules, and one draw needn't show every extreme that they name: `window_index`: within each aligned block of 4 window positions of a slide the entries are distinct indices into that block's 5 stored tiles.
All inputs are finite; a program needn't handle non-finite values.
Results may differ from a plain program's by a relative error of at most 0.013.
The roundings to bfloat16 on the way count: a program that leaves them out, or rounds other values in their place, can miss the bound.
Values may be sent and summed in bfloat16 or wider, within the bound.
A program may use at most 128 MiB of HBM per device.

v0:
```python
import jax
import jax.numpy as jnp
from jax import lax
from jax.sharding import PartitionSpec as P

C = 2048


exact_mode = lax.Precision.HIGHEST
eps_small = 1e-06


def pick_tiles(pool_maps, local_index):
    return jax.vmap(lambda slide_maps, slide_rows: jnp.take(slide_maps, slide_rows, axis=0))(
        pool_maps, local_index
    )


def direction_of(gradient, square_sum, entries):
    return gradient / (jnp.sqrt(square_sum / entries) + eps_small)


def local(
    residual_pool,
    inner_pool,
    window_index,
    labels,
    group_weight,
    expand_weight,
    attn_proj,
    attn_vector,
    classifier,
):
    slides_here = inner_pool.shape[0]
    map_side = inner_pool.shape[2]
    half_chan = inner_pool.shape[4]
    tiles_here = window_index.shape[1]
    group_width = group_weight.shape[2]
    groups_here = half_chan // group_width
    head_count = attn_vector.shape[1]
    class_count = classifier.shape[2]
    att_width = attn_proj.shape[2]
    cell_count = map_side * map_side
    tile_total = slides_here * tiles_here
    row_total = tile_total * cell_count
    picked_res = pick_tiles(residual_pool, window_index)
    picked_inner = pick_tiles(inner_pool, window_index)
    activated = jnp.maximum(picked_inner, 0).reshape(tile_total, map_side, map_side, half_chan)
    grouped = lax.conv_general_dilated(
        activated,
        group_weight,
        (1, 1),
        "SAME",
        dimension_numbers=("NHWC", "HWIO", "NHWC"),
        feature_group_count=groups_here,
        preferred_element_type=jnp.float32,
    )
    grouped_rows = grouped.reshape(row_total, half_chan)
    mid_rows = jnp.maximum(grouped_rows, 0.0).astype(jnp.bfloat16)
    residual_rows = picked_res.reshape(row_total, half_chan)
    mid_full = lax.all_gather(mid_rows, "chan", axis=1, tiled=True)
    pre_act = jnp.dot(mid_full, expand_weight, preferred_element_type=jnp.float32) + residual_rows
    pre_cells = pre_act.reshape(tile_total, cell_count, half_chan)
    features = (
        jnp.mean(jnp.maximum(pre_cells, 0.0), axis=1)
        .astype(jnp.bfloat16)
        .reshape(slides_here, tiles_here, half_chan)
    )
    features_f = features.astype(jnp.float32)
    class_f = classifier.astype(jnp.float32)
    vector_f = attn_vector.astype(jnp.float32)
    proj_part = jnp.einsum("stc,kca->stka", features, attn_proj, preferred_element_type=jnp.float32)
    projected = lax.psum(proj_part, "chan")
    tan_part = jnp.tanh(projected[:, :, 0])
    sig_part = jax.nn.sigmoid(projected[:, :, 1])
    gated = (tan_part * sig_part).astype(jnp.bfloat16)
    scores = jnp.einsum("sta,ah->sth", gated, attn_vector, preferred_element_type=jnp.float32)
    weights = jnp.exp(scores)
    local_sum = jnp.sum(weights, axis=1)
    weight_sum, pooled_sum = lax.psum(
        (local_sum, jnp.einsum("sth,stc->shc", weights, features_f, precision=exact_mode)), "tile"
    )
    pooled = pooled_sum / weight_sum[:, :, None]
    logits = lax.psum(jnp.einsum("shc,hck->sk", pooled, class_f, precision=exact_mode), "chan")
    exp_logits = jnp.exp(logits)
    exp_total = jnp.sum(exp_logits, axis=1)
    onehot = (labels[:, None] == jnp.arange(class_count, dtype=jnp.int32)[None, :]).astype(
        jnp.float32
    )
    slide_loss = jnp.log(exp_total) - jnp.sum(onehot * logits, axis=1)
    dlogits = exp_logits / exp_total[:, None] - onehot
    dpooled = jnp.einsum("sk,hck->shc", dlogits, class_f, precision=exact_mode)
    tile_dots, pool_dots = lax.psum(
        (
            jnp.einsum("shc,stc->sth", dpooled, features_f, precision=exact_mode),
            jnp.sum(dpooled * pooled, axis=2),
        ),
        "chan",
    )
    attn_share = weights / weight_sum[:, None, :]
    dscores = attn_share * (tile_dots - pool_dots[:, None, :])
    vector_part = jnp.einsum(
        "sta,sth->ah", gated.astype(jnp.float32), dscores, precision=exact_mode
    )
    dgated = jnp.einsum("sth,ah->sta", dscores, vector_f, precision=exact_mode)
    dgate = jnp.stack(
        [
            dgated * (1.0 - tan_part * tan_part) * sig_part,
            dgated * tan_part * sig_part * (1.0 - sig_part),
        ],
        axis=2,
    ).astype(jnp.bfloat16)
    proj_grad_part = jnp.einsum(
        "stc,stka->kca", features, dgate, preferred_element_type=jnp.float32
    )
    dfeatures = jnp.einsum("sth,shc->stc", attn_share, dpooled, precision=exact_mode) + jnp.einsum(
        "stka,kca->stc", dgate, attn_proj, preferred_element_type=jnp.float32
    )
    dpre_rows = (
        jnp.where(pre_cells > 0, dfeatures.reshape(tile_total, 1, half_chan) / cell_count, 0.0)
        .astype(jnp.bfloat16)
        .reshape(row_total, half_chan)
    )
    w3_part = lax.dot_general(
        mid_full, dpre_rows, (((0,), (0,)), ((), ())), preferred_element_type=jnp.float32
    )
    grad_w3 = lax.psum_scatter(w3_part, ("tile", "slide"), scatter_dimension=0, tiled=True)
    mid_part = lax.dot_general(
        dpre_rows, expand_weight, (((1,), (1,)), ((), ())), preferred_element_type=jnp.float32
    )
    dmid = lax.psum_scatter(
        mid_part.astype(jnp.bfloat16), "chan", scatter_dimension=1, tiled=True
    ).astype(jnp.float32)
    dgrouped = (
        jnp.where(grouped_rows > 0, dmid, 0.0)
        .astype(jnp.bfloat16)
        .reshape(row_total, groups_here, group_width)
    )
    padded = jnp.pad(activated, ((0, 0), (1, 1), (1, 1), (0, 0)))
    tap_rows = []
    for tap_y in range(3):
        tap_cols = []
        for tap_x in range(3):
            shifted = padded[:, tap_y : tap_y + map_side, tap_x : tap_x + map_side, :].reshape(
                row_total, groups_here, group_width
            )
            tap_cols.append(
                jnp.einsum(
                    "rgi,rgo->igo", shifted, dgrouped, preferred_element_type=jnp.float32
                ).reshape(group_width, half_chan)
            )
        tap_rows.append(jnp.stack(tap_cols))
    w2_part = jnp.stack(tap_rows)
    class_part = jnp.einsum("shc,sk->hck", pooled, dlogits, precision=exact_mode)
    grad_w2, grad_proj, grad_vector, grad_class = lax.psum(
        (w2_part, proj_grad_part, vector_part, class_part / lax.axis_size("tile")),
        ("tile", "slide"),
    )
    copies = lax.axis_size("tile") * lax.axis_size("slide")
    square_sums = lax.psum(
        (
            jnp.sum(grad_w3 * grad_w3),
            jnp.sum(grad_w2 * grad_w2) / copies,
            jnp.sum(grad_proj * grad_proj) / copies,
            jnp.sum(grad_vector * grad_vector) / (copies * lax.axis_size("chan")),
            jnp.sum(grad_class * grad_class) / copies,
        ),
        ("tile", "slide", "chan"),
    )
    dir_w3 = direction_of(grad_w3, square_sums[0], C * C)
    dir_w2 = direction_of(grad_w2, square_sums[1], 9 * group_width * C).astype(jnp.bfloat16)
    dir_proj = direction_of(grad_proj, square_sums[2], 2 * C * att_width).astype(jnp.bfloat16)
    dir_vector = direction_of(grad_vector, square_sums[3], att_width * head_count)
    dir_class = direction_of(grad_class, square_sums[4], head_count * C * class_count)
    return (slide_loss, dir_w2, dir_w3, dir_proj, dir_vector, dir_class)


def solution(mesh):
    return jax.shard_map(
        local,
        mesh=mesh,
        in_specs=(
            P(("parts", "slide"), "tile", None, None, "chan"),
            P(("parts", "slide"), "tile", None, None, "chan"),
            P(("parts", "slide"), "tile"),
            P(("parts", "slide")),
            P(None, None, None, "chan"),
            P(None, "chan"),
            P(None, "chan", None),
            P(),
            P(None, "chan", None),
        ),
        out_specs=(
            P(("parts", "slide")),
            P("parts", None, None, "chan"),
            P(("parts", "tile", "slide"), "chan"),
            P("parts", "chan", None),
            P("parts", None),
            P("parts", "chan", None),
        ),
        check_vma=False,
    )
```

profile of v0, /device:TPU:0, one launch (start us, length us, event | category | flops | bytes accessed | tf_op | source)
XLA Modules:
  0.0 684.1 jit_solution(13069880193377922007)
XLA Ops:
  8.8 5.9 gather_fusion
  18.3 5.9 gather_fusion.1
  29.6 6.1 reshape.152
  35.8 8.0 %shard_map.138 = bf16[3,3,64,32,64]{4,3,2,1,0:T(8,128)(2,1)} reshape(bf16[3,3,64,2048]{3,2,1,0:T(8,128)(2,1)} %param.15) | data formatting | bytes 4718592 | tf_op jit(solution)/shard_map/shard_map
  43.7 12.7 %maximum_convert_fusion = (bf16[8,7,7,32,64]{4,0,3,2,1:T(8,128)(2,1)S(1)}, f32[8,7,7,32,64]{4,0,3,2,1:T(8,128)}) fusion(bf16[3,3,64,32,64]{4,3,2,1,0:T(8,128)(2,1)} %shard_map.138, bf16[8,7,7,32,64]{4,3,2,1,0:T(8,128)(2,1)} %reshape.152), kind=kOutput, calls=%fused_computation.10 | convolution fusion | flops 758677504 | bytes 8781824 | tf_op jit(solution)/shard_map/conv_general_dilated | solution.py:49
  58.6 5.7 convert_element_type.52
  68.3 10.9 %broadcast_maximum_fusion = (f32[392,2048]{1,0:T(8,128)}, f32[392,2048]{1,0:T(8,128)}) fusion(f32[392,2048]{1,0:T(8,128)} %reshape.111, bf16[392,2048]{1,0:T(8,128)(2,1)} %convert_element_type.52, bf16[2048,2048]{1,0:T(8,128)(2,1)} %param.16), kind=kOutput, calls=%fused_computation.52 | convolution fusion | flops 3289939968 | bytes 19628032 | tf_op jit(solution)/shard_map/dot_general | solution.py:62
  87.5 11.4 %pad_slice_fusion.7 = (bf16[8,7,7,2048]{3,2,1,0:T(8,128)(2,1)}, bf16[8,7,7,2048]{3,2,1,0:T(8,128)(2,1)}, bf16[8,7,7,2048]{3,2,1,0:T(8,128)(2,1)}, bf16[8,7,7,204...) fusion(bf16[8,7,7,2048]{3,2,1,0:T(8,128)(2,1)} %bitcast.161), kind=kLoop, calls=%fused_computation.9 | loop fusion | bytes 14450688 | tf_op jit(solution)/shard_map/slice | solution.py:144
  98.9 5.1 broadcast_compare_fusion
  103.9 6.0 reshape.106
  117.7 6.0 reshape.102
  123.6 6.0 reshape.103
  129.6 6.0 reshape.104
  135.6 6.0 reshape.105
  141.5 6.0 reshape.107
  147.5 6.1 reshape.108
  153.6 5.9 reshape.109
  159.6 6.0 reshape.110
  165.6 13.4 %psum.90 = f32[2,8]{1,0:T(2,128)S(1)} all-reduce(f32[2,8]{1,0:T(2,128)S(1)} %get-tuple-element.45), channel_id=1, replica_groups=mesh['parts'=2,'tile'=4,'slide'=4,'chan'=1] {'tile'}, use_global_device_ids=true, to_apply=%region_3.5 | all-reduce | flops 16 | bytes 128 | tf_op jit(solution)/shard_map/psum | solution.py:80
  190.1 9.5 %select_convert_fusion = bf16[392,2048]{1,0:T(8,128)(2,1)} fusion(pred[392,2048]{1,0:T(8,128)(4,1)S(1)} %gt.11, bf16[2048,2048]{1,0:T(8,128)(2,1)} %param.16, bf16[392,2048]{1,0:T(8,128)(2,1)} %broadcast_in_dim.30, f32[392,2048]{1,0:T(8,128)} %get-tuple-element.44), kind=kOutput, calls=%fused_computation.38 | convolution fusion | flops 3293151232 | bytes 15613952 | tf_op jit(solution)/shard_map/dot_general | solution.py:128
  202.6 4.9 fusion.19
  208.6 4.9 fusion.17
  220.7 5.4 fusion.13
  227.3 4.9 fusion.9
  233.3 4.9 fusion.11
  245.5 5.1 fusion.5
  251.7 4.9 fusion.3
  264.3 10.8 %fusion.52 = f32[2048,2048]{1,0:T(8,128)} fusion(bf16[392,2048]{1,0:T(8,128)(2,1)S(1)} %copy-done.10, bf16[392,2048]{1,0:T(8,128)(2,1)} %broadcast_in_dim.30, f32[392,2048]{1,0:T(8,128)} %get-tuple-element.44), kind=kOutput, calls=%fused_computation.108 | convolution fusion | flops 3289939968 | bytes 23199744 | tf_op jit(solution)/shard_map/dot_general | solution.py:124
  275.3 32.8 %psum.96 = f32[256,8]{0,1:T(8,128)S(1)} all-reduce(f32[256,8]{0,1:T(8,128)S(1)} %convolution_bitcast_fusion.2), channel_id=1, replica_groups=mesh['parts'=2,'tile'=4,'slide'=4,'chan'=1] {'tile','slide'}, use_global_device_ids=true, to_apply=%region_16.18 | all-reduce | flops 2048 | bytes 16384 | tf_op jit(solution)/shard_map/psum | solution.py:155
  309.3 135.1 %all-reduce.8.cloned.1.call-done = (f32[3,3,64,2048]{3,2,1,0:T(8,128)}, f32[2,2048,256]{1,2,0:T(8,128)}, f32[8,2048,4]{1,2,0:T(4,128)}) async-done(((f32[3,3,64,2048]{3,2,1,0:T(8,128)}, f32[2,2048,256]{1,2,0:T(8,128)}, f32[8,2048,4]{1,2,0:T(4,128)}), (f32[3,3,64,2048]{3,2,1,0:T(8,128)}, f32[2,2048,256]{1,2,0:T(8,128)}, f32[8,2048,4]{1,2,0:T(4,128)})) %all-reduce.8.cloned.1.call-update) | async-done | bytes 9175056 | tf_op jit(solution)/shard_map/psum | solution.py:155
  455.2 171.8 %reduce-scatter.2.cloned.1.call-done = f32[128,2048]{1,0:T(8,128)} async-done(((f32[2048,2048]{1,0:T(8,128)}), f32[128,2048]{1,0:T(8,128)}) %reduce-scatter.2.cloned.1.call-update) | async-done | bytes 1048592 | tf_op jit(solution)/shard_map/reduce_scatter | solution.py:127
  629.6 32.2 %all-reduce.1 = (f32[]{:T(128)}, f32[]{:T(128)}, f32[]{:T(128)}, f32[]{:T(128)}, f32[]{:T(128)}) all-reduce(f32[]{:T(128)S(6)} %div.120, f32[]{:T(128)} %multiply_reduce_fusion.2, f32[]{:T(128)S(6)} %div.127, f32[]{:T(128)S(6)} %div.131, f32[]{:T(128)S(6)} %div.137), channel_id=1, replica_groups=mesh['parts'=2,'tile'=4,'slide'=4,'chan'=1] {'tile','slide','chan'}, use_global_device_ids=true, to_apply=%region_9.11 | all-reduce | flops 5 | bytes 40 | tf_op jit(solution)/shard_map/psum | solution.py:160
  (97 shorter events, 97.4 us)
Async XLA Ops:
  7.2 78.7 %copy-start = (bf16[2,2048,256]{2,1,0:T(8,128)(2,1)S(1)}, bf16[2,2048,256]{2,1,0:T(8,128)(2,1)}, u32[]{:S(2)}) copy-start(bf16[2,2048,256]{2,1,0:T(8,128)(2,1)} %param.17) | copy-start | bytes 6291460
  7.2 171.8 %all-reduce.6.cloned.1.call-start = ((), (), s32[]{:S(2)}) async-start(), calls=%async_computation.1 | async-start | bytes 262144 | tf_op jit(solution)/shard_map/psum | solution.py:80
  24.2 2.4 copy-start.2
  83.4 3.0 copy-start.12
  87.4 357.0 %all-reduce.8.cloned.1.call-start = ((), (), s32[]{:S(2)}) async-start(), calls=%async_computation.3 | async-start | bytes 18350080 | tf_op jit(solution)/shard_map/psum | solution.py:155
  159.6 20.4 %copy-start.13 = (s32[2]{0:T(128)S(1)}, s32[2]{0:T(128)}, u32[]{:S(2)}) copy-start(s32[2]{0:T(128)} %param.14) | copy-start | bytes 28
  159.6 20.4 %copy-start.14 = (bf16[8,2048,4]{1,2,0:T(4,128)(2,1)S(1)}, bf16[8,2048,4]{1,2,0:T(4,128)(2,1)}, u32[]{:S(2)}) copy-start(bf16[8,2048,4]{1,2,0:T(4,128)(2,1)} %param.19) | copy-start | bytes 393220
  256.6 2.8 copy-start.4
  257.7 1.7 copy-start.5
  257.8 1.7 copy-start.6
  257.8 1.8 copy-start.7
  257.8 2.0 copy-start.8
  257.8 2.1 copy-start.9
  262.9 1.4 copy-start.10
  262.9 364.1 %reduce-scatter.2.cloned.1.call-start = ((), (), s32[]{:S(2)}) async-start(), calls=%async_computation.2 | async-start | bytes 17825792 | tf_op jit(solution)/shard_map/reduce_scatter | solution.py:127
  448.6 5.2 copy-start.11
  671.1 5.2 copy-start.3
  671.1 6.3 copy-start.1
Sparse Core Ops, SparseCore 0:
  87.6 37.0 all-reduce.5
  263.0 181.3 all-reduce.7
  448.5 178.4 reduce-scatter.1
where the time goes:
time: 692 us; the launch traced here: 684 us
  waiting for transfers between devices  307 us (44%)
  local copies, waits for them, and re-layouts  140 us (20%)
  matrix products  97.5 us (14%)
  blocking collectives  78.4 us (11%)
  other arithmetic  40.2 us (6%)
  between operations  20.5 us (3%)
    reduce_scatter x1, waiting for transfers between devices, local(): lax.psum_scatter(w3_part, ('tile', 'slide'), scatter_dimension=0, tiled=T...  172 us
    psum x1, waiting for transfers between devices, local(): lax.psum((w2_part, proj_grad_part, vector_part, class_part / lax.axis_siz...  135 us
    reshape x9, local copies, waits for them, and re-layouts, local(): padded[:, tap_y:tap_y + map_side, tap_x:tap_x + map_side, :]  53.9 us
    dot_general x9, matrix products, local(): jnp.einsum('rgi,rgo->igo', shifted, dgrouped, preferred_element_type=jnp....  45 us
    psum x1, blocking collectives, local(): lax.psum((w2_part, proj_grad_part, vector_part, class_part / lax.axis_siz...  32.8 us
    psum x1, blocking collectives, local(): lax.psum((jnp.sum(grad_w3 * grad_w3), jnp.sum(grad_w2 * grad_w2) / copies...  32.2 us
    gather x5, local copies, waits for them, and re-layouts, pick_tiles(): jnp.take(slide_maps, slide_rows, axis=0)  17.9 us
  transfers between devices with their start and end apart: 3, of which 2 were waited for; matrix products, arithmetic and copies ran while one was open for 14% of the time, Pallas kernels for 0%

commit v1 on v0

v1 whole, which is shorter than its diff:
```python
import jax
import jax.numpy as jnp
from jax import lax
from jax.experimental import pallas as pl
from jax.experimental.pallas import tpu as pltpu
from jax.sharding import PartitionSpec as P

C = 2048


exact_mode = lax.Precision.HIGHEST
eps_small = 1e-06


BLOCK = 256
LIMIT = 40 * 1024 * 1024


def pick_rows(pool_maps, local_index, relu):
    stored = jnp.transpose(pool_maps, (1, 2, 3, 0, 4))
    spots = jnp.transpose(local_index)[None, None, :, :, None]
    picked = jnp.broadcast_to(
        stored[0][:, :, None], stored.shape[1:3] + (local_index.shape[1],) + stored.shape[3:]
    )
    for place in range(1, stored.shape[0]):
        picked = jnp.where(spots == place, stored[place][:, :, None], picked)
    if relu:
        picked = jnp.maximum(picked, 0)
    picked = jnp.pad(picked, ((0, 0), (0, 1), (0, 0), (0, 0), (0, 0)))
    return picked.reshape(-1, picked.shape[-1])


def fill_padded(x_ref, padded, edge):
    rows = x_ref.shape[0]
    zeros = jnp.zeros((edge, padded.shape[1]), padded.dtype)
    padded[0:edge, :] = zeros
    padded[edge + rows : edge + rows + edge, :] = zeros
    padded[edge : edge + rows, :] = x_ref[...]


def tap_slices(padded, rows, edge, line, cell):
    taps = []
    for tap_y in range(3):
        for tap_x in range(3):
            start = edge + (tap_y - 1) * line + (tap_x - 1) * cell
            taps.append(padded[start : start + rows, :])
    return taps


def conv_kernel(edge, line, cell, x_ref, w_ref, mid_ref, padded, dense):
    rows, width = x_ref.shape
    group = w_ref.shape[2]
    fill_padded(x_ref, padded, edge)
    own = lax.broadcasted_iota(jnp.int32, (width, width), 0) // group
    other = lax.broadcasted_iota(jnp.int32, (width, width), 1) // group
    same = (own == other).astype(jnp.float32).astype(jnp.bfloat16)
    for tap in range(9):
        small = w_ref[tap // 3, tap % 3]
        dense[tap * width : (tap + 1) * width, :] = (
            jnp.concatenate([small] * (width // group), axis=0) * same
        )
    lhs = jnp.concatenate(tap_slices(padded, rows, edge, line, cell), axis=1)
    grouped = jnp.dot(lhs, dense[...], preferred_element_type=jnp.float32)
    place = lax.broadcasted_iota(jnp.int32, (rows, width), 0) % line
    mid_ref[...] = jnp.where(place < line - cell, jnp.maximum(grouped, 0.0), 0.0).astype(
        jnp.bfloat16
    )


def grouped_forward(x_rows, group_weight, line, cell):
    rows, chans = x_rows.shape
    group = group_weight.shape[2]
    edge = line + 2 * cell
    return pl.pallas_call(
        lambda *refs: conv_kernel(edge, line, cell, *refs),
        grid=(chans // BLOCK,),
        in_specs=[
            pl.BlockSpec((rows, BLOCK), lambda i: (0, i)),
            pl.BlockSpec((3, 3, group, BLOCK), lambda i: (0, 0, 0, i)),
        ],
        out_specs=pl.BlockSpec((rows, BLOCK), lambda i: (0, i)),
        out_shape=jax.ShapeDtypeStruct((rows, chans), jnp.bfloat16),
        scratch_shapes=[
            pltpu.VMEM((rows + 2 * edge, BLOCK), jnp.bfloat16),
            pltpu.VMEM((9 * BLOCK, BLOCK), jnp.bfloat16),
        ],
        compiler_params=pltpu.CompilerParams(vmem_limit_bytes=LIMIT),
        name="grouped_forward",
    )(x_rows, group_weight)


def weight_kernel(edge, line, cell, x_ref, d_ref, out_ref, padded):
    rows, width = x_ref.shape
    group = out_ref.shape[2]
    fill_padded(x_ref, padded, edge)
    turned = jnp.transpose(d_ref[...])
    for tap, shifted in enumerate(tap_slices(padded, rows, edge, line, cell)):
        full = jnp.dot(turned, shifted, preferred_element_type=jnp.float32)
        own = jnp.concatenate(
            [
                full[at : at + group, at : at + group]
                for at in range(0, width, group)
            ],
            axis=0,
        )
        out_ref[tap // 3, tap % 3] = jnp.transpose(own).astype(out_ref.dtype)


def grouped_weight_grad(x_rows, d_rows, group, line, cell):
    rows, chans = x_rows.shape
    edge = line + 2 * cell
    return pl.pallas_call(
        lambda *refs: weight_kernel(edge, line, cell, *refs),
        grid=(chans // BLOCK,),
        in_specs=[
            pl.BlockSpec((rows, BLOCK), lambda i: (0, i)),
            pl.BlockSpec((rows, BLOCK), lambda i: (0, i)),
        ],
        out_specs=pl.BlockSpec((3, 3, group, BLOCK), lambda i: (0, 0, 0, i)),
        out_shape=jax.ShapeDtypeStruct((3, 3, group, chans), jnp.bfloat16),
        scratch_shapes=[pltpu.VMEM((rows + 2 * edge, BLOCK), jnp.bfloat16)],
        compiler_params=pltpu.CompilerParams(vmem_limit_bytes=LIMIT),
        name="grouped_weight_grad",
    )(x_rows, d_rows)


def direction_of(gradient, square_sum, entries):
    return gradient / (jnp.sqrt(square_sum / entries) + eps_small)


def local(
    residual_pool,
    inner_pool,
    window_index,
    labels,
    group_weight,
    expand_weight,
    attn_proj,
    attn_vector,
    classifier,
):
    slides_here = inner_pool.shape[0]
    map_side = inner_pool.shape[2]
    half_chan = inner_pool.shape[4]
    tiles_here = window_index.shape[1]
    group_width = group_weight.shape[2]
    head_count = attn_vector.shape[1]
    class_count = classifier.shape[2]
    att_width = attn_proj.shape[2]
    cell_count = map_side * map_side
    tile_total = slides_here * tiles_here
    line = (map_side + 1) * tile_total
    residual_rows = pick_rows(residual_pool, window_index, False)
    x_rows = pick_rows(inner_pool, window_index, True)
    mid_rows = grouped_forward(x_rows, group_weight, line, tile_total)
    mid_full = lax.all_gather(mid_rows, "chan", axis=1, tiled=True)
    pre_act = jnp.dot(mid_full, expand_weight, preferred_element_type=jnp.float32) + residual_rows
    pre_cells = pre_act.reshape(-1, tile_total, half_chan)
    features = (jnp.sum(jnp.maximum(pre_cells, 0.0), axis=0) / cell_count).astype(jnp.bfloat16)
    slide_devs = lax.axis_size("slide")
    tile_devs = lax.axis_size("tile")
    onehot_here = (
        labels[:, None] == jnp.arange(half_chan, dtype=jnp.int32)[None, :]
    ).astype(jnp.bfloat16)
    packet = jnp.concatenate([features, onehot_here], axis=0)
    gathered = lax.all_gather(packet, ("tile", "slide"), axis=0, tiled=False)
    slides_all = slide_devs * slides_here
    rows_all = tile_devs * slide_devs * tile_total
    feats = gathered[:, :tile_total].reshape(rows_all, half_chan)
    onehot = (
        gathered[:slide_devs, tile_total:, :class_count]
        .astype(jnp.float32)
        .reshape(slides_all, class_count)
    )
    row_at = jnp.arange(rows_all, dtype=jnp.int32)
    row_slide = (row_at // tile_total) % slide_devs * slides_here + row_at % slides_here
    select = (row_slide[:, None] == jnp.arange(slides_all, dtype=jnp.int32)[None, :]).astype(
        jnp.float32
    )
    feats_f = feats.astype(jnp.float32)
    class_f = jnp.transpose(classifier.astype(jnp.float32), (2, 0, 1))
    vector_f = attn_vector.astype(jnp.float32)
    proj_part = jnp.einsum("pc,kca->kpa", feats, attn_proj, preferred_element_type=jnp.float32)
    projected = lax.psum(proj_part, "chan")
    tan_part = jnp.tanh(projected[0])
    sig_part = jax.nn.sigmoid(projected[1])
    gated = (tan_part * sig_part).astype(jnp.bfloat16)
    scores = jnp.dot(gated, attn_vector, preferred_element_type=jnp.float32)
    weights = jnp.exp(scores)
    weight_sum = jnp.einsum("ps,ph->sh", select, weights, precision=exact_mode)
    spread = (select[:, :, None] * weights[:, None, :]).reshape(rows_all, slides_all * head_count)
    pooled_sum = jnp.einsum("pq,pc->qc", spread, feats_f, precision=exact_mode)
    pooled = pooled_sum.reshape(slides_all, head_count, half_chan) / weight_sum[:, :, None]
    logits = lax.psum(jnp.sum(pooled[:, None] * class_f[None], axis=(2, 3)), "chan")
    exp_logits = jnp.exp(logits)
    exp_total = jnp.sum(exp_logits, axis=1)
    loss_all = jnp.log(exp_total) - jnp.sum(onehot * logits, axis=1)
    dlogits = exp_logits / exp_total[:, None] - onehot
    dpooled = jnp.sum(dlogits[:, :, None, None] * class_f[None], axis=1)
    dots = jnp.einsum(
        "qc,pc->pq",
        dpooled.reshape(slides_all * head_count, half_chan),
        feats_f,
        precision=exact_mode,
    ).reshape(rows_all, slides_all, head_count)
    tile_dots, pool_dots = lax.psum(
        (jnp.sum(dots * select[:, :, None], axis=1), jnp.sum(dpooled * pooled, axis=2)), "chan"
    )
    row_sum = jnp.einsum("ps,sh->ph", select, weight_sum, precision=exact_mode)
    row_dots = jnp.einsum("ps,sh->ph", select, pool_dots, precision=exact_mode)
    attn_share = weights / row_sum
    dscores = attn_share * (tile_dots - row_dots)
    grad_vector = jnp.einsum("pa,ph->ah", gated.astype(jnp.float32), dscores, precision=exact_mode)
    dgated = jnp.einsum("ph,ah->pa", dscores, vector_f, precision=exact_mode)
    dgate = jnp.stack(
        [
            dgated * (1.0 - tan_part * tan_part) * sig_part,
            dgated * tan_part * sig_part * (1.0 - sig_part),
        ],
        axis=0,
    ).astype(jnp.bfloat16)
    grad_proj = jnp.einsum("pc,kpa->kca", feats, dgate, preferred_element_type=jnp.float32)
    grad_class = jnp.transpose(
        jnp.sum(dlogits[:, :, None, None] * pooled[:, None], axis=0), (1, 2, 0)
    )
    slide_at = lax.axis_index("slide")
    device_at = lax.axis_index("tile") * slide_devs + slide_at
    slide_loss = lax.dynamic_slice_in_dim(loss_all, slide_at * slides_here, slides_here)
    share_here = lax.dynamic_slice_in_dim(attn_share, device_at * tile_total, tile_total).reshape(
        tiles_here, slides_here, head_count
    )
    dpool_here = lax.dynamic_slice_in_dim(dpooled, slide_at * slides_here, slides_here)
    dgate_here = lax.dynamic_slice_in_dim(dgate, device_at * tile_total, tile_total, axis=1)
    dfeatures = jnp.einsum("tsh,shc->tsc", share_here, dpool_here, precision=exact_mode).reshape(
        tile_total, half_chan
    ) + jnp.einsum("kta,kca->tc", dgate_here, attn_proj, preferred_element_type=jnp.float32)
    dpre_rows = (
        jnp.where(pre_cells > 0, dfeatures[None] / cell_count, 0.0)
        .astype(jnp.bfloat16)
        .reshape(-1, half_chan)
    )
    w3_part = lax.dot_general(
        mid_full, dpre_rows, (((0,), (0,)), ((), ())), preferred_element_type=jnp.float32
    )
    grad_w3 = lax.psum_scatter(
        w3_part.astype(jnp.bfloat16), ("tile", "slide"), scatter_dimension=0, tiled=True
    ).astype(jnp.float32)
    mid_part = lax.dot_general(
        dpre_rows, expand_weight, (((1,), (1,)), ((), ())), preferred_element_type=jnp.float32
    )
    dmid = lax.psum_scatter(
        mid_part.astype(jnp.bfloat16), "chan", scatter_dimension=1, tiled=True
    ).astype(jnp.float32)
    d_rows = jnp.where(mid_rows > 0, dmid, 0.0).astype(jnp.bfloat16)
    w2_part = grouped_weight_grad(x_rows, d_rows, group_width, line, tile_total)
    grad_w2 = lax.psum(w2_part, ("tile", "slide")).astype(jnp.float32)
    w3_square = lax.psum(jnp.sum(grad_w3 * grad_w3), ("tile", "slide", "chan"))
    square_sums = (w3_square,) + lax.psum(
        (
            jnp.sum(grad_w2 * grad_w2),
            jnp.sum(grad_proj * grad_proj),
            jnp.sum(grad_vector * grad_vector) / lax.axis_size("chan"),
            jnp.sum(grad_class * grad_class),
        ),
        "chan",
    )
    dir_w3 = direction_of(grad_w3, square_sums[0], C * C)
    dir_w2 = direction_of(grad_w2, square_sums[1], 9 * group_width * C).astype(jnp.bfloat16)
    dir_proj = direction_of(grad_proj, square_sums[2], 2 * C * att_width).astype(jnp.bfloat16)
    dir_vector = direction_of(grad_vector, square_sums[3], att_width * head_count)
    dir_class = direction_of(grad_class, square_sums[4], head_count * C * class_count)
    return (slide_loss, dir_w2, dir_w3, dir_proj, dir_vector, dir_class)


def solution(mesh):
    return jax.shard_map(
        local,
        mesh=mesh,
        in_specs=(
            P(("parts", "slide"), "tile", None, None, "chan"),
            P(("parts", "slide"), "tile", None, None, "chan"),
            P(("parts", "slide"), "tile"),
            P(("parts", "slide")),
            P(None, None, None, "chan"),
            P(None, "chan"),
            P(None, "chan", None),
            P(),
            P(None, "chan", None),
        ),
        out_specs=(
            P(("parts", "slide")),
            P("parts", None, None, "chan"),
            P(("parts", "tile", "slide"), "chan"),
            P("parts", "chan", None),
            P("parts", None),
            P("parts", "chan", None),
        ),
        check_vma=False,
    )
```

time: 692 us -> 363 us (0.52); the launches traced: 684 us -> 362 us
  waiting for transfers between devices: 307 us -> 175 us
  local copies, waits for them, and re-layouts: 140 us -> 28.4 us
  matrix products: 97.5 us -> 37.3 us
  blocking collectives: 78.4 us -> 59.2 us
  Pallas kernels: 0 us -> 15.4 us
  other arithmetic: 40.2 us -> 29.2 us
    reduce_scatter x1, waiting for transfers between devices: 172 us -> 104 us  [local(): lax.psum_scatter(w3_part.astype(jnp.bfloat16), ('tile', 'slide'), scatter...]
    psum x2 -> x1, waiting for transfers between devices: 135 us -> 71.4 us  [local(): grad_w2 = lax.psum(w2_part, ('tile', 'slide')).astype(jnp.float32)]
    reshape x10 -> x2, local copies, waits for them, and re-layouts: 60 us -> 5.03 us  [the longest x1 4.98 us: pick_rows(): return picked.reshape(-1, picked.shape[-1])]
    psum x3 -> x1, blocking collectives: 78.4 us -> 32.8 us  [local(): w3_square = lax.psum(jnp.sum(grad_w3 * grad_w3), ('tile', 'slide', 'chan'))]
    dot_general x21 -> x12, matrix products: 53.6 us -> 9.71 us  [the longest x1 3.31 us: local(): jnp.einsum('pc,kpa->kca', feats, dgate, preferred_element_type=jnp.float32)]
    all_gather x0 -> x1, blocking collectives: none -> 26.4 us  [local(): gathered = lax.all_gather(packet, ('tile', 'slide'), axis=0, tiled=False)]
    another operation x10 -> x0, local copies, waits for them, and re-layouts: 18 us -> none  [the longest x9 10.1 us: local(): tap_rows.append(jnp.stack(tap_cols))]
    gather x5 -> x0, local copies, waits for them, and re-layouts: 17.9 us -> none  [pick_tiles(): jnp.take(slide_maps, slide_rows, axis=0)]
  transfers between devices with their start and end apart: 3 -> 2, of which waited for: 2 -> 2; matrix products, arithmetic and copies ran while one was open for 14% -> 7% of each run, Pallas kernels for 0% -> 0%
where the time goes in v1:
time: 363 us; the launch traced here: 362 us
  waiting for transfers between devices  175 us (48%)
  blocking collectives  59.2 us (16%)
  matrix products  37.3 us (10%)
  other arithmetic  29.2 us (8%)
  local copies, waits for them, and re-layouts  28.4 us (8%)
  between operations  17.8 us (5%)
  Pallas kernels  15.4 us (4%)
    reduce_scatter x1, waiting for transfers between devices, local(): lax.psum_scatter(w3_part.astype(jnp.bfloat16), ('tile', 'slide'), scatter...  104 us
    psum x1, waiting for transfers between devices, local(): grad_w2 = lax.psum(w2_part, ('tile', 'slide')).astype(jnp.float32)  71.4 us
    psum x1, blocking collectives, local(): w3_square = lax.psum(jnp.sum(grad_w3 * grad_w3), ('tile', 'slide', 'chan'))  32.8 us
    all_gather x1, blocking collectives, local(): gathered = lax.all_gather(packet, ('tile', 'slide'), axis=0, tiled=False)  26.4 us
    dot_general x1, matrix products, local(): jnp.dot(mid_full, expand_weight, preferred_element_type=jnp.float32)  9.88 us
    dot_general x1, matrix products, local(): lax.dot_general(mid_full, dpre_rows, (((0,), (0,)), ((), ())), preferred_...  9.06 us
    unnamed x38, local copies, waits for them, and re-layouts  8.94 us
    pallas_call x1, Pallas kernels, grouped_weight_grad(): pl.pallas_call(lambda *refs: weight_kernel(edge, line, cell, *refs), grid...  8.9 us
  transfers between devices with their start and end apart: 2, of which 2 were waited for; matrix products, arithmetic and copies ran while one was open for 7% of the time, Pallas kernels for 0%

profile of v1, /device:TPU:0, one launch (start us, length us, event | category | flops | bytes accessed | tf_op | source)
XLA Modules:
  0.0 362.4 jit_solution(16554255613066614304)
XLA Ops:
  7.2 0.8 compare_bitcast_fusion
  9.2 0.9 convert_bitcast_fusion
  10.3 4.4 %slice_bitcast_fusion.5 = (bf16[7,7,2,2048]{3,2,1,0:T(2,128)(2,1)S(1)}, bf16[7,7,2,2048]{3,2,1,0:T(2,128)(2,1)S(1)}, bf16[7,7,2,2048]{3,2,1,0:T(2,128)(2,1)S(1)}...) fusion(bf16[5,7,7,2,2048]{4,3,2,1,0:T(2,128)(2,1)} %bitcast.116, ...), kind=kLoop, calls=%fused_computation.48 | loop fusion | bytes 8028160 | tf_op jit(solution)/shard_map/jit(_where)/broadcast_in_dim | solution.py:26
  14.8 5.3 %fusion.6 = (bf16[7,7,4,2,2048]{4,3,2,1,0:T(2,128)(2,1)S(1)}, bf16[7,7,4,2,2048]{4,3,2,1,0:T(2,128)(2,1)}) fusion(pred[4,2]{1,0:T(4,128)(4,1)S(1)} %copy.44, pred[4,2]{1,0:T(4,128)(4,1)S(1)} %copy.45, pred[4,2]{1,0:T(4,128)(4,1)S(1)} %copy.46, pred[4,2]{1,0:T(4,128)(4,1)S(1)} %copy.47, bf16[7,7,2,2048]{3,2,1,0:T(2,128)(2,1)S(1)} %get-tuple-element.59, ...), kind=kLoop, calls=%fused_computation.31 | loop fusion | flops 7225344 | bytes 7225376 | tf_op jit(solution)/shard_map/max | solution.py:28
  20.1 3.0 pad.7
  23.1 5.0 %reshape.157.refs_0_ = bf16[448,2048]{1,0:T(8,128)(2,1)} reshape(bf16[7,8,4,2,2048]{4,3,2,1,0:T(2,128)(2,1)} %pad.7) | data formatting | bytes 3670016 | tf_op jit(solution)/shard_map/reshape | solution.py:30
  28.1 5.2 %pad_convert_fusion = f32[7,8,4,2,2048]{4,3,2,1,0:T(2,128)} fusion(bf16[7,7,4,2,2048]{4,3,2,1,0:T(2,128)(2,1)} %get-tuple-element.45), kind=kLoop, calls=%fused_computation.30 | loop fusion | flops 917504 | bytes 5275648 | tf_op jit(solution)/shard_map/convert_element_type | solution.py:157
  33.3 5.5 %reshape.162 = f32[448,2048]{1,0:T(8,128)} reshape(f32[7,8,4,2,2048]{4,3,2,1,0:T(2,128)} %pad_convert_fusion) | data formatting | bytes 7340032 | tf_op jit(solution)/shard_map/convert_element_type | solution.py:157
  38.8 1.5 copy-done.2
  40.3 1.7 copy-done.4
  42.0 6.5 %grouped_forward.1 = bf16[448,2048]{1,0:T(8,128)(2,1)S(1)} custom-call(bf16[448,2048]{1,0:T(8,128)(2,1)S(1)} %copy-done.2, bf16[3,3,64,2048]{3,2,1,0:T(8,128)(2,1)S(1)} %copy-done.4), custom_call_target="tpu_custom_call" | custom-call | tf_op jit(solution)/shard_map/grouped_forward/pallas_call | solution.py:74
  48.5 9.9 %bitcast_reduce_fusion = (f32[8,2048]{1,0:T(8,128)S(1)}, f32[448,2048]{1,0:T(8,128)}) fusion(f32[448,2048]{1,0:T(8,128)S(1)} %copy-done.9, bf16[448,2048]{1,0:T(8,128)(2,1)S(1)} %grouped_forward.1, bf16[2048,2048]{1,0:T(8,128)(2,1)} %param.14), kind=kOutput, calls=%fused_computation.9 | convolution fusion | flops 3760832512 | bytes 17629184 | tf_op jit(solution)/shard_map/dot_general | solution.py:157
  58.4 26.4 %all-gather.1 = bf16[16,10,2048]{2,1,0:T(8,128)(2,1)S(1)} all-gather(bf16[1,10,2048]{2,1,0:T(8,128)(2,1)S(1)} %maximum_bitcast_fusion), channel_id=2, replica_groups=mesh['parts'=2,'tile'=4,'slide'=4,'chan'=1] {'tile','slide'}, dimensions={0}, use_global_device_ids=true | all-gather | bytes 696320 | tf_op jit(solution)/shard_map/all_gather | solution.py:166
  86.6 1.1 multiply_reduce_fusion.1
  89.5 0.9 fusion.20
  90.4 1.2 convolution_bitcast_fusion.1
  91.7 1.5 fusion.4
  93.2 8.6 %select_convert_fusion.refs_1_ = bf16[448,2048]{1,0:T(8,128)(2,1)S(1)} fusion(bf16[448,2048]{1,0:T(8,128)(2,1)S(1)} %copy-done.6, bf16[2048,2048]{1,0:T(8,128)(2,1)} %param.14, f32[448,2048]{1,0:T(8,128)} %get-tuple-element.51, bf16[8,2048]{1,0:T(8,128)(2,1)S(1)} %fusion.4), kind=kOutput, calls=%fused_computation.10 | convolution fusion | flops 3764518912 | bytes 15761408 | tf_op jit(solution)/shard_map/dot_general | solution.py:248
  101.8 8.9 %grouped_weight_grad.1 = bf16[3,3,64,2048]{3,2,1,0:T(8,128)(2,1)} custom-call(bf16[448,2048]{1,0:T(8,128)(2,1)S(1)} %copy-done.3, bf16[448,2048]{1,0:T(8,128)(2,1)S(1)} %select_convert_fusion.refs_1_), custom_call_target="tpu_custom_call" | custom-call | tf_op jit(solution)/shard_map/grouped_weight_grad/pallas_call | solution.py:112
  111.0 1.2 copy-done.7
  112.2 9.1 %convolution_convert_fusion = bf16[2048,2048]{1,0:T(8,128)(2,1)} fusion(bf16[448,2048]{1,0:T(8,128)(2,1)S(1)} %copy-done.7, f32[448,2048]{1,0:T(8,128)} %get-tuple-element.51, bf16[8,2048]{1,0:T(8,128)(2,1)S(1)} %fusion.4), kind=kOutput, calls=%fused_computation | convolution fusion | flops 3764125696 | bytes 13926400 | tf_op jit(solution)/shard_map/dot_general | solution.py:242
  123.9 0.9 copy.54
  126.3 3.3 multiply_reduce_fusion
  130.3 2.7 fusion.5
  133.0 2.5 copy.53
  136.1 71.4 %all-reduce.4.cloned.1.call-done = bf16[3,3,64,2048]{3,2,1,0:T(8,128)(2,1)} async-done(((bf16[3,3,64,2048]{3,2,1,0:T(8,128)(2,1)}), bf16[3,3,64,2048]{3,2,1,0:T(8,128)(2,1)}) %all-reduce.4.cloned.1.call-update) | async-done | bytes 2359312 | tf_op jit(solution)/shard_map/psum | solution.py:256
  207.4 3.5 fusion
  211.6 103.6 %reduce-scatter.2.cloned.1.call-done = bf16[128,2048]{1,0:T(8,128)(2,1)} async-done(((bf16[2048,2048]{1,0:T(8,128)(2,1)}), bf16[128,2048]{1,0:T(8,128)(2,1)}) %reduce-scatter.2.cloned.1.call-update) | async-done | bytes 524304 | tf_op jit(solution)/shard_map/reduce_scatter | solution.py:245
  315.2 2.1 fusion.9
  317.2 3.7 %fusion.1 = bf16[3,3,64,2048]{3,2,1,0:T(8,128)(2,1)} fusion(bf16[3,3,64,2048]{3,2,1,0:T(8,128)(2,1)} %all-reduce.4.cloned.1.call-done, f32[]{:T(128)S(6)} %add.118), kind=kLoop, calls=%fused_computation.4 | loop fusion | flops 3538944 | bytes 4718596 | tf_op jit(solution)/shard_map/convert_element_type | solution.py:268
  321.0 32.8 %psum.15 = f32[]{:T(128)} all-reduce(f32[]{:T(128)} %fusion.9), channel_id=1, replica_groups=mesh['parts'=2,'tile'=4,'slide'=4,'chan'=1] {'tile','slide','chan'}, use_global_device_ids=true, to_apply=%region_11.12 | all-reduce | flops 1 | bytes 8 | tf_op jit(solution)/shard_map/psum | solution.py:257
  354.5 1.1 convert_divide_fusion.1
  (72 shorter events, 8.7 us)
Async XLA Ops:
  7.2 77.6 %copy-start = (bf16[2,2048,256]{2,1,0:T(8,128)(2,1)S(1)}, bf16[2,2048,256]{2,1,0:T(8,128)(2,1)}, u32[]{:S(2)}) copy-start(bf16[2,2048,256]{2,1,0:T(8,128)(2,1)} %param.15) | copy-start | bytes 6291460
  7.2 200.2 %all-reduce.4.cloned.1.call-start = ((), (), s32[]{:S(2)}) async-start(), calls=%async_computation.1 | async-start | bytes 4718592 | tf_op jit(solution)/shard_map/psum | solution.py:256
  38.8 1.5 copy-start.2
  40.3 1.7 copy-start.4
  42.0 6.5 %copy-start.9 = (f32[448,2048]{1,0:T(8,128)S(1)}, f32[448,2048]{1,0:T(8,128)}, u32[]{:S(2)}) copy-start(f32[448,2048]{1,0:T(8,128)} %reshape.162) | copy-start | bytes 11010052
  48.4 9.9 %copy-start.5 = (bf16[448,2048]{1,0:T(8,128)(2,1)}, bf16[448,2048]{1,0:T(8,128)(2,1)S(1)}, u32[]{:S(2)}) copy-start(bf16[448,2048]{1,0:T(8,128)(2,1)S(1)} %grouped_forward.1) | copy-start | bytes 5505028
  58.4 26.9 %copy-start.15 = (bf16[256,8]{0,1:T(8,128)(2,1)S(1)}, bf16[256,8]{0,1:T(8,128)(2,1)}, u32[]{:S(2)}) copy-start(bf16[256,8]{0,1:T(8,128)(2,1)} %param.16) | copy-start | bytes 12292
  85.2 1.3 copy-start.12
  86.5 1.1 copy-start.16
  87.7 0.8 copy-start.8
  87.7 1.8 copy-start.13
  91.7 1.5 copy-start.6
  93.2 8.6 %copy-start.3 = (bf16[448,2048]{1,0:T(8,128)(2,1)S(1)}, bf16[448,2048]{1,0:T(8,128)(2,1)}, u32[]{:S(2)}) copy-start(bf16[448,2048]{1,0:T(8,128)(2,1)} %reshape.157.refs_0_) | copy-start | bytes 5505028
  110.7 1.5 copy-start.7
  110.7 204.4 %reduce-scatter.2.cloned.1.call-start = ((), (), s32[]{:S(2)}) async-start(), calls=%async_computation.2 | async-start | bytes 8912896 | tf_op jit(solution)/shard_map/reduce_scatter | solution.py:245
  121.3 0.7 copy-start.17
  121.3 1.3 copy-start.10
  121.3 5.0 %copy-start.14 = (bf16[1,128,256]{2,1,0:T(8,128)(2,1)S(1)}, bf16[1,128,256]{2,1,0:T(8,128)(2,1)}, u32[]{:S(2)}) copy-start(bf16[1,128,256]{2,1,0:T(8,128)(2,1)} %get-tuple-element.43) | copy-start | bytes 196612
  315.2 40.4 %copy-start.1 = (bf16[2,2048,256]{2,1,0:T(8,128)(2,1)S(1)}, bf16[2,2048,256]{2,1,0:T(8,128)(2,1)}, u32[]{:S(2)}) copy-start(bf16[2,2048,256]{2,1,0:T(8,128)(2,1)} %param.15) | copy-start | bytes 6291460
  317.2 37.3 %copy-start.11 = (bf16[128,2048]{1,0:T(8,128)(2,1)S(1)}, bf16[128,2048]{1,0:T(8,128)(2,1)}, u32[]{:S(2)}) copy-start(bf16[128,2048]{1,0:T(8,128)(2,1)} %reduce-scatter.2.cloned.1.call-done) | copy-start | bytes 1572868
Sparse Core Ops, SparseCore 0:
  110.9 96.5 all-reduce.3
  211.5 103.6 reduce-scatter.1

commit v2 on v1

--- a/solution.py
+++ b/solution.py
@@ -13,6 +13,8 @@
 
 
 BLOCK = 256
+LANES = 128
+CHUNKS = 4
 LIMIT = 40 * 1024 * 1024
 
 
@@ -26,16 +28,20 @@
         picked = jnp.where(spots == place, stored[place][:, :, None], picked)
     if relu:
         picked = jnp.maximum(picked, 0)
-    picked = jnp.pad(picked, ((0, 0), (0, 1), (0, 0), (0, 0), (0, 0)))
+    picked = lax.optimization_barrier(picked)
     return picked.reshape(-1, picked.shape[-1])
 
 
-def fill_padded(x_ref, padded, edge):
-    rows = x_ref.shape[0]
-    zeros = jnp.zeros((edge, padded.shape[1]), padded.dtype)
-    padded[0:edge, :] = zeros
-    padded[edge + rows : edge + rows + edge, :] = zeros
-    padded[edge : edge + rows, :] = x_ref[...]
+def fill_padded(x_ref, padded, edge, line, cell):
+    filled = line - cell
+    for at in range(x_ref.shape[0] // filled):
+        start = edge + at * line
+        padded[start : start + filled, :] = x_ref[at * filled : (at + 1) * filled, :]
+        padded[start + filled : start + line, :] = jnp.zeros((cell, padded.shape[1]), padded.dtype)
+    if edge:
+        zeros = jnp.zeros((edge, padded.shape[1]), padded.dtype)
+        padded[0:edge, :] = zeros
+        padded[padded.shape[0] - edge :, :] = zeros
 
 
 def tap_slices(padded, rows, edge, line, cell):
@@ -48,9 +54,11 @@
 
 
 def conv_kernel(edge, line, cell, x_ref, w_ref, mid_ref, padded, dense):
-    rows, width = x_ref.shape
+    width = x_ref.shape[1]
+    rows = padded.shape[0] - 2 * edge
+    filled = line - cell
     group = w_ref.shape[2]
-    fill_padded(x_ref, padded, edge)
+    fill_padded(x_ref, padded, edge, line, cell)
     own = lax.broadcasted_iota(jnp.int32, (width, width), 0) // group
     other = lax.broadcasted_iota(jnp.int32, (width, width), 1) // group
     same = (own == other).astype(jnp.float32).astype(jnp.bfloat16)
@@ -61,10 +69,11 @@
         )
     lhs = jnp.concatenate(tap_slices(padded, rows, edge, line, cell), axis=1)
     grouped = jnp.dot(lhs, dense[...], preferred_element_type=jnp.float32)
-    place = lax.broadcasted_iota(jnp.int32, (rows, width), 0) % line
-    mid_ref[...] = jnp.where(place < line - cell, jnp.maximum(grouped, 0.0), 0.0).astype(
-        jnp.bfloat16
-    )
+    mid = jnp.maximum(grouped, 0.0)
+    for at in range(rows // line):
+        mid_ref[at * filled : (at + 1) * filled, :] = mid[
+            at * line : at * line + filled, :
+        ].astype(jnp.bfloat16)
 
 
 def grouped_forward(x_rows, group_weight, line, cell):
@@ -81,7 +90,7 @@
         out_specs=pl.BlockSpec((rows, BLOCK), lambda i: (0, i)),
         out_shape=jax.ShapeDtypeStruct((rows, chans), jnp.bfloat16),
         scratch_shapes=[
-            pltpu.VMEM((rows + 2 * edge, BLOCK), jnp.bfloat16),
+            pltpu.VMEM((rows // (line - cell) * line + 2 * edge, BLOCK), jnp.bfloat16),
             pltpu.VMEM((9 * BLOCK, BLOCK), jnp.bfloat16),
         ],
         compiler_params=pltpu.CompilerParams(vmem_limit_bytes=LIMIT),
@@ -89,11 +98,14 @@
     )(x_rows, group_weight)
 
 
-def weight_kernel(edge, line, cell, x_ref, d_ref, out_ref, padded):
-    rows, width = x_ref.shape
-    group = out_ref.shape[2]
-    fill_padded(x_ref, padded, edge)
-    turned = jnp.transpose(d_ref[...])
+def weight_kernel(edge, line, cell, x_ref, d_ref, out_ref, padded, d_padded):
+    width = x_ref.shape[1]
+    rows = padded.shape[0] - 2 * edge
+    part_width = out_ref.shape[2]
+    group = out_ref.shape[1] // 9
+    fill_padded(x_ref, padded, edge, line, cell)
+    fill_padded(d_ref, d_padded, 0, line, cell)
+    turned = jnp.transpose(d_padded[...])
     for tap, shifted in enumerate(tap_slices(padded, rows, edge, line, cell)):
         full = jnp.dot(turned, shifted, preferred_element_type=jnp.float32)
         own = jnp.concatenate(
@@ -103,7 +115,11 @@
             ],
             axis=0,
         )
-        out_ref[tap // 3, tap % 3] = jnp.transpose(own).astype(out_ref.dtype)
+        turned_back = jnp.transpose(own).astype(out_ref.dtype)
+        for part in range(width // part_width):
+            out_ref[part, tap * group : (tap + 1) * group, :] = turned_back[
+                :, part * part_width : (part + 1) * part_width
+            ]
 
 
 def grouped_weight_grad(x_rows, d_rows, group, line, cell):
@@ -116,12 +132,279 @@
             pl.BlockSpec((rows, BLOCK), lambda i: (0, i)),
             pl.BlockSpec((rows, BLOCK), lambda i: (0, i)),
         ],
-        out_specs=pl.BlockSpec((3, 3, group, BLOCK), lambda i: (0, 0, 0, i)),
-        out_shape=jax.ShapeDtypeStruct((3, 3, group, chans), jnp.bfloat16),
-        scratch_shapes=[pltpu.VMEM((rows + 2 * edge, BLOCK), jnp.bfloat16)],
+        out_specs=pl.BlockSpec((BLOCK // LANES, 9 * group, LANES), lambda i: (i, 0, 0)),
+        out_shape=jax.ShapeDtypeStruct((chans // LANES, 9 * group, LANES), jnp.bfloat16),
+        scratch_shapes=[
+            pltpu.VMEM((rows // (line - cell) * line + 2 * edge, BLOCK), jnp.bfloat16),
+            pltpu.VMEM((rows // (line - cell) * line, BLOCK), jnp.bfloat16),
+        ],
         compiler_params=pltpu.CompilerParams(vmem_limit_bytes=LIMIT),
         name="grouped_weight_grad",
     )(x_rows, d_rows)
+
+
+def places():
+    tile_at, slide_at = lax.axis_index("tile"), lax.axis_index("slide")
+    return tile_at, slide_at // 2, slide_at % 2
+
+
+def remote(src, dst, sems, item, step, tile_to, x_to, core_to):
+    send, recv = sems
+    return pltpu.make_async_remote_copy(
+        src_ref=src,
+        dst_ref=dst,
+        send_sem=send.at[item, step],
+        recv_sem=recv.at[item, step],
+        device_id={"tile": tile_to, "slide": x_to * 2 + core_to},
+        device_id_type=pl.DeviceIdType.MESH,
+    )
+
+
+def entry_barrier():
+    z, x, c = places()
+    barrier = pltpu.get_barrier_semaphore()
+    peers = [(z, x, 1 - c), (z, 1 - x, c)] + [((z + d) % 4, x, c) for d in (1, 2, 3)]
+    for tile_to, x_to, core_to in peers:
+        pl.semaphore_signal(
+            barrier,
+            inc=1,
+            device_id={"tile": tile_to, "slide": x_to * 2 + core_to},
+            device_id_type=pl.DeviceIdType.MESH,
+        )
+    pl.semaphore_wait(barrier, len(peers))
+
+
+def gather_tile(gat, sems, item):
+    z, x, c = places()
+    own = gat.at[z, x, c]
+    return [remote(own, own, sems, item, d - 1, (z + d) % 4, x, c) for d in (1, 2, 3)]
+
+
+def gather_x(gat, sems, item):
+    z, x, c = places()
+    own = gat.at[:, x, c]
+    return [remote(own, own, sems, item, 3, z, 1 - x, c)]
+
+
+def gather_core(gat, sems, item):
+    z, x, c = places()
+    own = gat.at[:, :, c]
+    return [remote(own, own, sems, item, 4, z, x, 1 - c)]
+
+
+def start_all(copies):
+    for copy in copies:
+        copy.start()
+    return copies
+
+
+def wait_all(copies):
+    for copy in copies:
+        copy.wait()
+
+
+def gather_kernel(own_ref, gat, send, recv):
+    z, x, c = places()
+    sems = (send, recv)
+    entry_barrier()
+    gat[z, x, c] = own_ref[...]
+    wait_all(start_all(gather_tile(gat, sems, 0)))
+    wait_all(start_all(gather_x(gat, sems, 0)))
+    wait_all(start_all(gather_core(gat, sems, 0)))
+
+
+def gather_packets(packet):
+    return pl.pallas_call(
+        gather_kernel,
+        in_specs=[pl.BlockSpec(memory_space=pltpu.VMEM)],
+        out_specs=pl.BlockSpec(memory_space=pltpu.VMEM),
+        out_shape=jax.ShapeDtypeStruct((4, 2, 2) + packet.shape, packet.dtype),
+        scratch_shapes=[pltpu.SemaphoreType.DMA((1, 5)), pltpu.SemaphoreType.DMA((1, 5))],
+        compiler_params=pltpu.CompilerParams(
+            collective_id=1, has_side_effects=True, vmem_limit_bytes=LIMIT
+        ),
+        name="gather_packets",
+    )(packet)
+
+
+def reduce_kernel(
+    entries3,
+    entries2,
+    w3_ref,
+    w2_ref,
+    dir3_ref,
+    dir2_ref,
+    core3,
+    side3,
+    line3,
+    core2,
+    side2,
+    line2,
+    gat,
+    squares,
+    send,
+    recv,
+):
+    z, x, c = places()
+    sems = (send, recv)
+    wide = w3_ref.shape[4] // CHUNKS
+    f32 = jnp.float32
+
+    def parts(item):
+        if item == 0:
+            return w2_ref.at, core2, side2, line2, slice(None)
+        at = item - 1
+        return w3_ref.at, core3.at[at], side3.at[at], line3.at[at], slice(at * wide, (at + 1) * wide)
+
+    def first(item):
+        whole, got, _, _, cols = parts(item)
+        return [remote(whole[:, :, 1 - c, :, cols], got, sems, item, 0, z, x, 1 - c)]
+
+    def second(item):
+        _, got, other, _, _ = parts(item)
+        return [remote(got.at[:, 1 - x], other, sems, item, 1, z, 1 - x, c)]
+
+    def third(item):
+        _, _, other, ends, _ = parts(item)
+        return [
+            remote(other.at[(z + d) % 4], ends.at[d - 1], sems, item, 1 + d, (z + d) % 4, x, c)
+            for d in (1, 2, 3)
+        ]
+
+    def after_first(item):
+        _, got, _, _, cols = parts(item)
+        wait_all(copies1[item])
+        source = w2_ref if item == 0 else w3_ref
+
+        def add(at, carry):
+            row, col = at // 2, at % 2
+            got[row, col] = (
+                source[row, col, c, :, cols].astype(f32) + got[row, col].astype(f32)
+            ).astype(jnp.bfloat16)
+            return carry
+
+        lax.fori_loop(0, 8, add, 0)
+        copies2[item] = start_all(second(item))
+
+    def after_second(item):
+        _, got, other, _, _ = parts(item)
+        wait_all(copies2[item])
+
+        def add(row, carry):
+            other[row] = (got[row, x].astype(f32) + other[row].astype(f32)).astype(jnp.bfloat16)
+            return carry
+
+        lax.fori_loop(0, 4, add, 0)
+        copies3[item] = start_all(third(item))
+
+    def total(item):
+        _, _, other, ends, _ = parts(item)
+        wait_all(copies3[item])
+        return ((other[z].astype(f32) + ends[0].astype(f32)) + ends[1].astype(f32)) + ends[
+            2
+        ].astype(f32)
+
+    def fold(values):
+        flat = values.reshape(values.shape[0] // 8, 8, values.shape[1])
+        flat = jnp.sum(flat * flat, axis=0)
+        out = flat[:, 0:LANES]
+        for at in range(LANES, flat.shape[1], LANES):
+            out = out + flat[:, at : at + LANES]
+        return out
+
+    def finish(item):
+        value = total(item)
+        dir3_ref[:, (item - 1) * wide : item * wide] = value
+        return fold(value)
+
+    def scale(tile_sum, entries):
+        return 1.0 / (jnp.sqrt(jnp.sum(tile_sum, keepdims=True) / entries) + eps_small)
+
+    copies1, copies2, copies3 = {}, {}, {}
+    last = CHUNKS
+    entry_barrier()
+    for item in range(last + 1):
+        copies1[item] = start_all(first(item))
+    after_first(0)
+    after_first(1)
+    after_second(0)
+    after_first(2)
+    after_second(1)
+    gat[z, x, c] = total(0).astype(jnp.bfloat16)
+    gathering = start_all(gather_tile(gat, sems, last + 1))
+    after_first(3)
+    after_second(2)
+    square = finish(1)
+    wait_all(gathering)
+    gathering = start_all(gather_x(gat, sems, last + 1))
+    after_first(4)
+    after_second(3)
+    square = square + finish(2)
+    wait_all(gathering)
+    gathering = start_all(gather_core(gat, sems, last + 1))
+    after_second(4)
+    square = square + finish(3)
+    wait_all(gathering)
+
+    def square2(at, carry):
+        return carry + fold(gat[at // 4, at // 2 % 2, at % 2].astype(f32))
+
+    scale2 = scale(lax.fori_loop(0, 16, square2, jnp.zeros((8, LANES), f32)), entries2)
+    for at in range(16):
+        dir2_ref[:, at * LANES : (at + 1) * LANES] = (
+            gat[at // 4, at // 2 % 2, at % 2].astype(f32) * scale2
+        ).astype(jnp.bfloat16)
+    square = square + finish(4)
+    squares[0] = square
+    item = last + 2
+    wait_all(start_all([remote(squares.at[0], squares.at[1], sems, item, 0, z, x, 1 - c)]))
+    squares[2] = squares[0] + squares[1]
+    wait_all(start_all([remote(squares.at[2], squares.at[3], sems, item, 1, z, 1 - x, c)]))
+    squares[4] = squares[2] + squares[3]
+    wait_all(
+        start_all(
+            [
+                remote(squares.at[4], squares.at[4 + d], sems, item, 1 + d, (z + d) % 4, x, c)
+                for d in (1, 2, 3)
+            ]
+        )
+    )
+    scale3 = scale((squares[4] + squares[5]) + (squares[6] + squares[7]), entries3)
+    dir3_ref[...] = dir3_ref[...] * scale3
+
+
+def reduce_directions(w3_part, w2_part, entries3, entries2):
+    depth, chans = w3_part.shape
+    rows3 = depth // 16
+    rows2 = w2_part.shape[1]
+    wide = chans // CHUNKS
+    half = jnp.bfloat16
+    vmem = pl.BlockSpec(memory_space=pltpu.VMEM)
+    return pl.pallas_call(
+        lambda *refs: reduce_kernel(entries3, entries2, *refs),
+        in_specs=[vmem, vmem],
+        out_specs=[vmem, vmem],
+        out_shape=[
+            jax.ShapeDtypeStruct((rows3, chans), jnp.float32),
+            jax.ShapeDtypeStruct((rows2, chans), half),
+        ],
+        scratch_shapes=[
+            pltpu.VMEM((CHUNKS, 4, 2, rows3, wide), half),
+            pltpu.VMEM((CHUNKS, 4, rows3, wide), half),
+            pltpu.VMEM((CHUNKS, 3, rows3, wide), half),
+            pltpu.VMEM((4, 2, rows2, LANES), half),
+            pltpu.VMEM((4, rows2, LANES), half),
+            pltpu.VMEM((3, rows2, LANES), half),
+            pltpu.VMEM((4, 2, 2, rows2, LANES), half),
+            pltpu.VMEM((8, 8, LANES), jnp.float32),
+            pltpu.SemaphoreType.DMA((CHUNKS + 3, 5)),
+            pltpu.SemaphoreType.DMA((CHUNKS + 3, 5)),
+        ],
+        compiler_params=pltpu.CompilerParams(
+            collective_id=2, has_side_effects=True, vmem_limit_bytes=LIMIT
+        ),
+        name="reduce_directions",
+    )(w3_part.reshape(4, 2, 2, rows3, chans), w2_part.reshape(4, 2, 2, rows2, LANES))
 
 
 def direction_of(gradient, square_sum, entries):
@@ -163,7 +446,15 @@
         labels[:, None] == jnp.arange(half_chan, dtype=jnp.int32)[None, :]
     ).astype(jnp.bfloat16)
     packet = jnp.concatenate([features, onehot_here], axis=0)
-    gathered = lax.all_gather(packet, ("tile", "slide"), axis=0, tiled=False)
+    own_kernels = (
+        slide_devs == 4 and tile_devs == 4 and lax.axis_size("chan") == 1 and half_chan == 16 * LANES
+    )
+    if own_kernels:
+        spare = -packet.shape[0] % 16
+        gathered = gather_packets(jnp.pad(packet, ((0, spare), (0, 0))))
+        gathered = gathered.reshape((-1,) + gathered.shape[3:])[:, : packet.shape[0]]
+    else:
+        gathered = lax.all_gather(packet, ("tile", "slide"), axis=0, tiled=False)
     slides_all = slide_devs * slides_here
     rows_all = tile_devs * slide_devs * tile_total
     feats = gathered[:, :tile_total].reshape(rows_all, half_chan)
@@ -242,9 +533,6 @@
     w3_part = lax.dot_general(
         mid_full, dpre_rows, (((0,), (0,)), ((), ())), preferred_element_type=jnp.float32
     )
-    grad_w3 = lax.psum_scatter(
-        w3_part.astype(jnp.bfloat16), ("tile", "slide"), scatter_dimension=0, tiled=True
-    ).astype(jnp.float32)
     mid_part = lax.dot_general(
         dpre_rows, expand_weight, (((1,), (1,)), ((), ())), preferred_element_type=jnp.float32
     )
@@ -253,22 +541,31 @@
     ).astype(jnp.float32)
     d_rows = jnp.where(mid_rows > 0, dmid, 0.0).astype(jnp.bfloat16)
     w2_part = grouped_weight_grad(x_rows, d_rows, group_width, line, tile_total)
-    grad_w2 = lax.psum(w2_part, ("tile", "slide")).astype(jnp.float32)
-    w3_square = lax.psum(jnp.sum(grad_w3 * grad_w3), ("tile", "slide", "chan"))
-    square_sums = (w3_square,) + lax.psum(
+    entries2 = 9 * group_width * C
+    if own_kernels:
+        dir_w3, dir_w2 = reduce_directions(w3_part.astype(jnp.bfloat16), w2_part, C * C, entries2)
+        dir_w2 = dir_w2.reshape(3, 3, group_width, half_chan)
+    else:
+        grad_w3 = lax.psum_scatter(
+            w3_part.astype(jnp.bfloat16), ("tile", "slide"), scatter_dimension=0, tiled=True
+        ).astype(jnp.float32)
+        grad_w2 = lax.psum(w2_part, ("tile", "slide")).astype(jnp.float32)
+        w3_square = lax.psum(jnp.sum(grad_w3 * grad_w3), ("tile", "slide", "chan"))
+        w2_square = lax.psum(jnp.sum(grad_w2 * grad_w2), "chan")
+        dir_w3 = direction_of(grad_w3, w3_square, C * C)
+        dir_w2 = direction_of(grad_w2, w2_square, entries2).astype(jnp.bfloat16)
+        dir_w2 = jnp.transpose(dir_w2, (1, 0, 2)).reshape(3, 3, group_width, half_chan)
+    square_sums = lax.psum(
         (
-            jnp.sum(grad_w2 * grad_w2),
             jnp.sum(grad_proj * grad_proj),
             jnp.sum(grad_vector * grad_vector) / lax.axis_size("chan"),
             jnp.sum(grad_class * grad_class),
         ),
         "chan",
     )
-    dir_w3 = direction_of(grad_w3, square_sums[0], C * C)
-    dir_w2 = direction_of(grad_w2, square_sums[1], 9 * group_width * C).astype(jnp.bfloat16)
-    dir_proj = direction_of(grad_proj, square_sums[2], 2 * C * att_width).astype(jnp.bfloat16)
-    dir_vector = direction_of(grad_vector, square_sums[3], att_width * head_count)
-    dir_class = direction_of(grad_class, square_sums[4], head_count * C * class_count)
+    dir_proj = direction_of(grad_proj, square_sums[0], 2 * C * att_width).astype(jnp.bfloat16)
+    dir_vector = direction_of(grad_vector, square_sums[1], att_width * head_count)
+    dir_class = direction_of(grad_class, square_sums[2], head_count * C * class_count)
     return (slide_loss, dir_w2, dir_w3, dir_proj, dir_vector, dir_class)
 
 

time: 363 us -> 228 us (0.63)
  waiting for transfers between devices: 175 us -> 0 us
  Pallas kernels: 15.4 us -> 140 us
  blocking collectives: 59.2 us -> 0 us
  between operations: 17.8 us -> 2.99 us
  other arithmetic: 29.2 us -> 17.7 us
  local copies, waits for them, and re-layouts: 28.4 us -> 33.9 us
  matrix products: 37.3 us -> 33.1 us
    pallas_call x0 -> x2, Pallas kernels: none -> 125 us  [the longest x1 106 us: reduce_directions(): pl.pallas_call(lambda *refs: reduce_kernel(entries3, entries2, *refs), in...]
    reduce_scatter x1 -> x0, waiting for transfers between devices: 104 us -> none  [local(): lax.psum_scatter(w3_part.astype(jnp.bfloat16), ('tile', 'slide'), scatter...]
    psum x1 -> x0, waiting for transfers between devices: 71.4 us -> none  [local(): grad_w2 = lax.psum(w2_part, ('tile', 'slide')).astype(jnp.float32)]
    psum x1 -> x0, blocking collectives: 32.8 us -> none  [local(): w3_square = lax.psum(jnp.sum(grad_w3 * grad_w3), ('tile', 'slide', 'chan'))]
    all_gather x1 -> x0, blocking collectives: 26.4 us -> none  [local(): gathered = lax.all_gather(packet, ('tile', 'slide'), axis=0, tiled=False)]
    unnamed x38, local copies, waits for them, and re-layouts: 8.94 us -> 16.9 us
    convert_element_type x3 -> x1, other arithmetic: 11.6 us -> 3.99 us  [local(): direction_of(grad_proj, square_sums[0], 2 * C * att_width)]
    reduce_sum x2 -> x0, other arithmetic: 5.55 us -> none  [the longest x1 3.48 us: local(): jnp.sum(grad_w2 * grad_w2)]
  transfers between devices with their start and end apart: 2 -> 0, of which waited for: 2 -> 0; matrix products, arithmetic and copies ran while one was open for 7% -> 0% of each run, Pallas kernels for 0% -> 0%
where the time goes in v2:
time: 228 us; the launch traced here: 227 us
  Pallas kernels  140 us (61%)
  local copies, waits for them, and re-layouts  33.9 us (15%)
  matrix products  33.1 us (15%)
  other arithmetic  17.7 us (8%)
  between operations  2.99 us (1%)
    pallas_call x1, Pallas kernels, reduce_directions(): pl.pallas_call(lambda *refs: reduce_kernel(entries3, entries2, *refs), in...  106 us
    pallas_call x1, Pallas kernels, gather_packets(): pl.pallas_call(gather_kernel, in_specs=[pl.BlockSpec(memory_space=pltpu.V...  19.4 us
    unnamed x38, local copies, waits for them, and re-layouts  16.9 us
    dot_general x1, matrix products, local(): jnp.dot(mid_full, expand_weight, preferred_element_type=jnp.float32)  9.13 us
    pallas_call x1, Pallas kernels, grouped_weight_grad(): pl.pallas_call(lambda *refs: weight_kernel(edge, line, cell, *refs), grid...  8.1 us
    dot_general x1, matrix products, local(): lax.dot_general(mid_full, dpre_rows, (((0,), (0,)), ((), ())), preferred_...  7.13 us
    dot_general x1, matrix products, local(): lax.dot_general(dpre_rows, expand_weight, (((1,), (1,)), ((), ())), prefe...  7.1 us
    pallas_call x1, Pallas kernels, grouped_forward(): pl.pallas_call(lambda *refs: conv_kernel(edge, line, cell, *refs), grid=(...  6.43 us

profile of v2, /device:TPU:0, one launch (start us, length us, event | category | flops | bytes accessed | tf_op | source)
XLA Modules:
  0.0 227.3 jit_solution(5439895407454886022)
XLA Ops:
  0.6 1.1 convert_bitcast_fusion
  1.9 0.7 compare_convert_fusion
  2.6 0.7 compare_bitcast_fusion
  3.7 4.4 %slice_bitcast_fusion.5 = (bf16[7,7,2,2048]{3,2,1,0:T(2,128)(2,1)S(1)}, bf16[7,7,2,2048]{3,2,1,0:T(2,128)(2,1)S(1)}, bf16[7,7,2,2048]{3,2,1,0:T(2,128)(2,1)S(1)}...) fusion(bf16[5,7,7,2,2048]{4,3,2,1,0:T(2,128)(2,1)} %bitcast.127, ...), kind=kLoop, calls=%fused_computation.40 | loop fusion | bytes 8028160 | tf_op jit(solution)/shard_map/jit(_where)/broadcast_in_dim | solution.py:28
  8.2 5.4 %fusion.4 = (bf16[7,7,4,2,2048]{4,3,2,1,0:T(2,128)(2,1)}, bf16[7,7,4,2,2048]{4,3,2,1,0:T(2,128)(2,1)}) fusion(pred[4,2]{1,0:T(4,128)(4,1)S(1)} %copy.35, pred[4,2]{1,0:T(4,128)(4,1)S(1)} %copy.36, pred[4,2]{1,0:T(4,128)(4,1)S(1)} %copy.37, pred[4,2]{1,0:T(4,128)(4,1)S(1)} %copy.38, bf16[7,7,2,2048]{3,2,1,0:T(2,128)(2,1)S(1)} %get-tuple-element.57, ...), kind=kLoop, calls=%fused_computation.26 | loop fusion | flops 7225344 | bytes 7225376 | tf_op jit(solution)/shard_map/max | solution.py:30
  13.6 5.0 %reshape.178 = f32[392,2048]{1,0:T(8,128)} reshape(bf16[7,7,4,2,2048]{4,3,2,1,0:T(2,128)(2,1)} %get-tuple-element.43) | data formatting | bytes 4816896 | tf_op jit(solution)/shard_map/convert_element_type | solution.py:440
  18.5 4.7 %reshape.169.refs_0_ = bf16[392,2048]{1,0:T(8,128)(2,1)} reshape(bf16[7,7,4,2,2048]{4,3,2,1,0:T(2,128)(2,1)} %get-tuple-element.42) | data formatting | bytes 3211264 | tf_op jit(solution)/shard_map/reshape | solution.py:32
  23.2 1.4 copy-done.1
  24.6 1.7 copy-done.5
  26.3 6.4 %grouped_forward.1 = bf16[392,2048]{1,0:T(8,128)(2,1)S(1)} custom-call(bf16[392,2048]{1,0:T(8,128)(2,1)S(1)} %copy-done.1, bf16[3,3,64,2048]{3,2,1,0:T(8,128)(2,1)S(1)} %copy-done.5), custom_call_target="tpu_custom_call" | custom-call | tf_op jit(solution)/shard_map/grouped_forward/pallas_call | solution.py:83
  32.7 9.1 %bitcast_reduce_fusion = (f32[8,2048]{1,0:T(8,128)S(1)}, f32[392,2048]{1,0:T(8,128)}) fusion(f32[392,2048]{1,0:T(8,128)S(1)} %copy-done.11, bf16[392,2048]{1,0:T(8,128)(2,1)S(1)} %grouped_forward.1, bf16[2048,2048]{1,0:T(8,128)(2,1)} %param.14), kind=kOutput, calls=%fused_computation.5 | convolution fusion | flops 3290726400 | bytes 16482304 | tf_op jit(solution)/shard_map/dot_general | solution.py:440
  41.9 19.4 %gather_packets.1 = bf16[4,2,2,16,2048]{4,3,2,1,0:T(8,128)(2,1)S(1)} custom-call(bf16[16,2048]{1,0:T(8,128)(2,1)S(1)} %fusion.20.own_ref), custom_call_target="tpu_custom_call" | custom-call | tf_op jit(solution)/shard_map/gather_packets/pallas_call | solution.py:217
  62.9 0.8 copy-done.10
  64.9 2.4 %multiply_reduce_fusion.1 = (f32[4,8,2048]{2,1,0:T(8,128)}, f32[8,8,2048]{2,1,0:T(8,128)}) fusion(f32[8,4]{1,0:T(8,128)S(1)} %divide_subtract_fusion, f32[8,8,2048]{2,1,0:T(8,128)} %copy-done.10, f32[4,8,2048]{2,1,0:T(8,128)S(1)} %copy.39), kind=kLoop, calls=%fused_computation.22 | loop fusion | flops 1900544 | bytes 1572992 | tf_op jit(solution)/shard_map/reduce_sum | solution.py:515
  67.6 1.2 convolution_bitcast_fusion.1
  68.8 0.7 copy.42
  69.4 0.9 reshape.174
  70.3 1.8 fusion.5
  72.2 1.5 multiply_reduce_fusion.4
  74.8 7.1 %convolution_convert_fusion = bf16[2048,2048]{1,0:T(8,128)(2,1)} fusion(bf16[392,2048]{1,0:T(8,128)(2,1)S(1)} %copy-done.7, f32[392,2048]{1,0:T(8,128)S(1)} %copy-done.16, bf16[8,2048]{1,0:T(8,128)(2,1)S(1)} %fusion.2), kind=kOutput, calls=%fused_computation | convolution fusion | flops 3294134272 | bytes 13238272 | tf_op jit(solution)/shard_map/dot_general | solution.py:533
  81.9 7.1 %select_convert_fusion.refs_1_ = bf16[392,2048]{1,0:T(8,128)(2,1)S(1)} fusion(bf16[392,2048]{1,0:T(8,128)(2,1)S(1)} %copy-done.7, bf16[2048,2048]{1,0:T(8,128)(2,1)} %param.14, f32[392,2048]{1,0:T(8,128)S(1)} %copy-done.16, bf16[8,2048]{1,0:T(8,128)(2,1)S(1)} %fusion.2), kind=kOutput, calls=%fused_computation.6 | convolution fusion | flops 3293954048 | bytes 14843904 | tf_op jit(solution)/shard_map/dot_general | solution.py:536
  89.1 8.1 %grouped_weight_grad.1 = bf16[16,576,128]{2,1,0:T(8,128)(2,1)S(1)} custom-call(bf16[392,2048]{1,0:T(8,128)(2,1)S(1)} %copy-done.2, bf16[392,2048]{1,0:T(8,128)(2,1)S(1)} %select_convert_fusion.refs_1_), custom_call_target="tpu_custom_call" | custom-call | tf_op jit(solution)/shard_map/grouped_weight_grad/pallas_call | solution.py:128
  97.2 3.4 %copy-done.3 = bf16[2048,2048]{1,0:T(8,128)(2,1)S(1)} copy-done((bf16[2048,2048]{1,0:T(8,128)(2,1)S(1)}, bf16[2048,2048]{1,0:T(8,128)(2,1)}, u32[]{:S(2)}) %copy-start.3) | copy-done | bytes 8388632
  100.6 105.7 %reduce_directions.1 = (f32[128,2048]{1,0:T(8,128)S(1)}, bf16[576,2048]{1,0:T(8,128)(2,1)S(1)}) custom-call(bf16[4,2,2,128,2048]{4,3,2,1,0:T(8,128)(2,1)S(1)} %bitcast.119, bf16[4,2,2,576,128]{4,3,2,1,0:T(8,128)(2,1)S(1)} %bitcast.118), custom_call_target="tpu_custom_call" | custom-call | tf_op jit(solution)/shard_map/reduce_directions/pallas_call | solution.py:383
  206.3 3.6 %multiply_reduce_fusion = (f32[]{:T(128)}, f32[2,256,2048]{2,1,0:T(8,128)}) fusion(bf16[16,16,2048]{2,1,0:T(8,128)(2,1)S(1)} %bitcast.125, bf16[1,128,256]{2,1,0:T(8,128)(2,1)S(1)} %get-tuple-element.40, bf16[1,128,256]{2,1,0:T(8,128)(2,1)S(1)} %get-tuple-element.41), kind=kOutput, calls=%fused_computation.2 | convolution fusion | flops 270598144 | bytes 4849668 | tf_op jit(solution)/shard_map/pc,kpa->kca/dot_general | solution.py:513
  210.6 4.0 %fusion.3 = bf16[2,2048,256]{1,2,0:T(8,128)(2,1)} fusion(f32[2,256,2048]{2,1,0:T(8,128)} %get-tuple-element.51, f32[]{:T(128)S(6)} %add.103), kind=kLoop, calls=%fused_computation.25 | loop fusion | flops 2097152 | bytes 6291460 | tf_op jit(solution)/shard_map/convert_element_type | solution.py:566
  214.6 4.0 %copy.44 = bf16[2,2048,256]{2,1,0:T(8,128)(2,1)} copy(bf16[2,2048,256]{1,2,0:T(8,128)(2,1)} %fusion.3) | data formatting | bytes 4194304
  218.6 0.7 multiply_reduce_fusion.6
  220.6 0.7 multiply_reduce_fusion.5
  222.0 0.9 copy.45
  222.9 3.4 %copy.51 = bf16[3,3,64,2048]{3,2,1,0:T(8,128)(2,1)} copy(bf16[3,3,64,2048]{3,2,1,0:T(8,128)(2,1)} %bitcast.126) | data formatting | bytes 4718592
  226.3 1.0 copy.52
  (60 shorter events, 5.5 us)
Async XLA Ops:
  0.6 60.7 %copy-start = (bf16[2,2048,256]{2,1,0:T(8,128)(2,1)S(1)}, bf16[2,2048,256]{2,1,0:T(8,128)(2,1)}, u32[]{:S(2)}) copy-start(bf16[2,2048,256]{2,1,0:T(8,128)(2,1)} %param.15) | copy-start | bytes 6291460
  23.2 1.4 copy-start.1
  24.6 1.7 copy-start.5
  26.3 6.4 %copy-start.11 = (f32[392,2048]{1,0:T(8,128)S(1)}, f32[392,2048]{1,0:T(8,128)}, u32[]{:S(2)}) copy-start(f32[392,2048]{1,0:T(8,128)} %reshape.178) | copy-start | bytes 9633796
  32.7 9.1 %copy-start.6 = (bf16[392,2048]{1,0:T(8,128)(2,1)}, bf16[392,2048]{1,0:T(8,128)(2,1)S(1)}, u32[]{:S(2)}) copy-start(bf16[392,2048]{1,0:T(8,128)(2,1)S(1)} %grouped_forward.1) | copy-start | bytes 4816900
  41.9 20.0 %copy-start.15 = (bf16[256,8]{0,1:T(8,128)(2,1)S(1)}, bf16[256,8]{0,1:T(8,128)(2,1)}, u32[]{:S(2)}) copy-start(bf16[256,8]{0,1:T(8,128)(2,1)} %param.16) | copy-start | bytes 12292
  61.8 0.7 copy-start.13
  62.9 0.8 copy-start.10
  67.3 6.6 %copy-start.14 = (f32[2,128,256]{2,1,0:T(8,128)S(1)}, f32[2,128,256]{2,1,0:T(8,128)}, u32[]{:S(2)}) copy-start(f32[2,128,256]{2,1,0:T(8,128)} %copy-done.13) | copy-start | bytes 786436
  70.3 4.5 %copy-start.16 = (f32[392,2048]{1,0:T(8,128)S(1)}, f32[392,2048]{1,0:T(8,128)}, u32[]{:S(2)}) copy-start(f32[392,2048]{1,0:T(8,128)} %get-tuple-element.49) | copy-start | bytes 9633796
  72.2 2.6 %copy-start.7 = (bf16[392,2048]{1,0:T(8,128)(2,1)S(1)}, bf16[392,2048]{1,0:T(8,128)(2,1)}, u32[]{:S(2)}) copy-start(bf16[392,2048]{1,0:T(8,128)(2,1)} %copy-done.6) | copy-start | bytes 4816900
  81.9 7.1 %copy-start.2 = (bf16[392,2048]{1,0:T(8,128)(2,1)S(1)}, bf16[392,2048]{1,0:T(8,128)(2,1)}, u32[]{:S(2)}) copy-start(bf16[392,2048]{1,0:T(8,128)(2,1)} %reshape.169.refs_0_) | copy-start | bytes 4816900
  97.2 3.4 %copy-start.3 = (bf16[2048,2048]{1,0:T(8,128)(2,1)S(1)}, bf16[2048,2048]{1,0:T(8,128)(2,1)}, u32[]{:S(2)}) copy-start(bf16[2048,2048]{1,0:T(8,128)(2,1)} %convolution_convert_fusion) | copy-start | bytes 25165828
  206.3 3.6 %copy-start.4 = (bf16[576,2048]{1,0:T(8,128)(2,1)}, bf16[576,2048]{1,0:T(8,128)(2,1)S(1)}, u32[]{:S(2)}) copy-start(bf16[576,2048]{1,0:T(8,128)(2,1)S(1)} %get-tuple-element.8) | copy-start | bytes 7077892
  206.3 3.6 %copy-start.8 = (f32[128,2048]{1,0:T(8,128)}, f32[128,2048]{1,0:T(8,128)S(1)}, u32[]{:S(2)}) copy-start(f32[128,2048]{1,0:T(8,128)S(1)} %get-tuple-element.67) | copy-start | bytes 3145732
  214.6 6.0 %copy-start.12 = (f32[4,8,2048]{2,1,0:T(8,128)S(1)}, f32[4,8,2048]{2,1,0:T(8,128)}, u32[]{:S(2)}) copy-start(f32[4,8,2048]{2,1,0:T(8,128)} %get-tuple-element.28) | copy-start | bytes 786436
  222.9 3.5 %copy-start.9 = (f32[128,2048]{1,0:T(8,128)S(1)}, f32[128,2048]{1,0:T(8,128)}, u32[]{:S(2)}) copy-start(f32[128,2048]{1,0:T(8,128)} %copy-done.8) | copy-start | bytes 3145732
